TPU v7x, 32 devices: a whole 2x2x4 slice. The times are simulated.
32 devices in a mesh: circ: 4 (over z), rad: 4 (over y, x), ax: 2 (over core).
Axes of the slice: x: 2, y: 2, z: 4, core: 2. Of those that a mesh axis runs over, the one named last changes fastest.
Arguments:
- state: float32 [5, 16, 32, 512], P(None, 'ax', 'rad', 'circ'), may hold values from -6 to 6
- eddy: float32 [16, 32, 512], P('ax', 'rad', 'circ'), may hold values from 0.02 to 0.2
- offsets: int32 [4], replicated, may hold values from 0 to 3, as said below
- stencil_index: int32 [2, 4, 128, 4], replicated, may hold values from 0 to 127
- stencil_weight: float32 [2, 4, 128, 4], replicated, may hold values from 0.1 to 1
Outputs:
- advanced: float32 [5, 16, 32, 512], P(None, 'ax', 'rad', 'circ')
Inputs may be any that keep to these rules, and one draw needn't show every extreme that they name: Among the sections' offsets are 2, 3 and 0.
All inputs are finite; a program needn't handle non-finite values.
Results may differ from a plain program's by a relative error of at most 0.00005.
Values sent between devices are 32-bit elements; how exact they have to be, the bound alone decides.
A program may use at most 64 MiB of HBM per device.

v0:
```python
import jax
import jax.numpy as jnp
from jax import lax
from jax.sharding import PartitionSpec as P

AXIAL_MACH = 0.4
STEP_SIZE = 0.3


def passed_along(x, axis, by):
    count = lax.axis_size(axis)
    return lax.ppermute(x, axis, [(i, (i + by) % count) for i in range(count)])


def swapped(value, axis, apart):
    mask = 2**apart
    pairs = [(source, source ^ mask) for source in range(lax.axis_size(axis))]
    return lax.ppermute(value, axis, pairs)


def padded(x, sides, width, wrap):
    for axis, dim in sides:
        count, length = (lax.axis_size(axis), x.shape[dim])
        up = [(i, (i + 1) % count) for i in range(count if wrap else count - 1)]
        down = [(j, i) for i, j in up]
        last = lax.slice_in_dim(x, length - width, length, axis=dim)
        leading = lax.slice_in_dim(x, 0, width, axis=dim)
        before = lax.ppermute(last, axis, up)
        after = lax.ppermute(leading, axis, down)
        x = jnp.concatenate([before, x, after], axis=dim)
    return x


def interp_matrix(index_rows, weight_rows):
    width = index_rows.shape[0]
    onehot = (index_rows[:, :, None] == jnp.arange(width, dtype=jnp.int32)[None, None, :]).astype(
        jnp.float32
    )
    normed = weight_rows / jnp.sum(weight_rows, axis=1, keepdims=True)
    return jnp.sum(normed[:, :, None] * onehot, axis=1)


def tendency(
    center, circ_low, circ_high, radial_low, radial_high, axial_low, axial_high, swirl, eddy
):
    diff_circ = 0.5 * (circ_high - circ_low)
    diff_radial = 0.5 * (radial_high - radial_low)
    diff_axial = 0.5 * (axial_high - axial_low)
    laplace = (
        circ_high + circ_low + (radial_high + radial_low) + (axial_high + axial_low) - 6.0 * center
    )
    advect = swirl * diff_circ + AXIAL_MACH * diff_axial
    diverge = diff_circ[1] + diff_radial[2] + diff_axial[3]
    flux = jnp.stack([diverge, diff_circ[4], diff_radial[4], diff_axial[4], diverge])
    return -advect - flux + eddy[None] * laplace


def facing_ghost(field, offset_now, index_section, weight_section):
    sectors = lax.axis_size("circ")
    is_rotor = lax.axis_index("ax") == 1
    plane_out = jnp.where(is_rotor, field[:, 0], field[:, -1])
    amount = jnp.where(is_rotor, offset_now, (sectors - offset_now) % sectors)
    carried = plane_out
    for bit_level in range((sectors - 1).bit_length()):
        moved = passed_along(carried, "circ", 1 << bit_level)
        carried = jnp.where((amount >> bit_level) % 2 == 1, moved, carried)
    received = swapped(carried, "ax", 0)
    table_side = lax.axis_index("ax")
    matrix = interp_matrix(index_section[table_side], weight_section[table_side])
    width = received.shape[-1]
    flat_rows = received.reshape(-1, width)
    ghost = jnp.dot(
        flat_rows, matrix.T, precision=lax.Precision.HIGHEST, preferred_element_type=jnp.float32
    )
    return ghost.reshape(received.shape)


def section_tendency(field, eddy, offset_now, index_section, weight_section):
    is_rotor = lax.axis_index("ax") == 1
    circ_padded = padded(field, (("circ", 3),), 1, True)
    radial_padded = padded(field, (("rad", 2),), 1, False)
    ghost = facing_ghost(field, offset_now, index_section, weight_section)
    zero_plane = jnp.zeros_like(ghost)
    below = jnp.where(is_rotor, ghost, zero_plane)[:, None]
    above = jnp.where(is_rotor, zero_plane, ghost)[:, None]
    axial_low = jnp.concatenate([below, field[:, :-1]], axis=1)
    axial_high = jnp.concatenate([field[:, 1:], above], axis=1)
    swirl = jnp.where(is_rotor, -0.3, 0.2).astype(jnp.float32)
    return tendency(
        field,
        circ_padded[..., :-2],
        circ_padded[..., 2:],
        radial_padded[:, :, :-2],
        radial_padded[:, :, 2:],
        axial_low,
        axial_high,
        swirl,
        eddy,
    )


def local(state, eddy, offsets, stencil_index, stencil_weight):

    def slope(field, section):
        return section_tendency(
            field, eddy, offsets[section], stencil_index[:, section], stencil_weight[:, section]
        )

    slope_one = slope(state, 0)
    slope_two = slope(state + 0.5 * STEP_SIZE * slope_one, 1)
    slope_three = slope(state + 0.5 * STEP_SIZE * slope_two, 2)
    slope_four = slope(state + STEP_SIZE * slope_three, 3)
    return state + STEP_SIZE / 6.0 * (slope_one + 2.0 * slope_two + 2.0 * slope_three + slope_four)


def solution(mesh):
    return jax.shard_map(
        local,
        mesh=mesh,
        in_specs=(P(None, "ax", "rad", "circ"), P("ax", "rad", "circ"), P(), P(), P()),
        out_specs=P(None, "ax", "rad", "circ"),
        check_vma=False,
    )
```

profile of v0, /device:TPU:0, one launch (start us, length us, event | category | flops | bytes accessed | tf_op | source)
XLA Modules:
  0.0 93.3 jit_solution(12625657827502762632)
XLA Ops:
  0.8 3.0 %collective-permute-start.2 = (f32[5,8,128]{2,1,0:T(8,128)S(1)}, f32[5,8,128]{2,1,0:T(8,128)S(1)}, u32[]{:S(2)}, u32[]{:S(2)}) collective-permute-start(f32[5,8,128]{2,1,0:T(8,128)S(1)} %fusion.19), channel_id=1, source_target_pairs={{0,8},{8,16},{16,24},{24,0},{1,9},{9,17},{17,25},{25,1},{2,10},{10... | collective-permute-start | bytes 61448 | tf_op jit(solution)/shard_map/ppermute | solution.py:12
  4.8 3.4 %collective-permute-start.6 = (f32[5,8,1,128]{3,2,0,1:T(1,128)S(1)}, f32[5,8,1,128]{3,2,0,1:T(1,128)S(1)}, u32[]{:S(2)}, u32[]{:S(2)}) collective-permute-start(f32[5,8,1,128]{3,2,0,1:T(1,128)S(1)} %get-tuple-element.39), channel_id=1, source_target_pairs={{0,2},{2,4},{4,6},{1,3},{3,5},{5,7},{8,10},{10,12},{12,14},{9,11},... | collective-permute-start | bytes 61448 | tf_op jit(solution)/shard_map/ppermute | solution.py:28
  8.2 1.3 %collective-permute-start.5 = (f32[5,8,1,128]{3,2,0,1:T(1,128)S(1)}, f32[5,8,1,128]{3,2,0,1:T(1,128)S(1)}, u32[]{:S(2)}, u32[]{:S(2)}) collective-permute-start(f32[5,8,1,128]{3,2,0,1:T(1,128)S(1)} %get-tuple-element.40), channel_id=1, source_target_pairs={{2,0},{4,2},{6,4},{3,1},{5,3},{7,5},{10,8},{12,10},{14,12},{11,9},... | collective-permute-start | bytes 61448 | tf_op jit(solution)/shard_map/ppermute | solution.py:29
  10.7 1.6 %collective-permute-start.1 = (f32[5,8,8,1]{3,2,0,1:T(8,128)S(1)}, f32[5,8,8,1]{3,2,0,1:T(8,128)S(1)}, u32[]{:S(2)}, u32[]{:S(2)}) collective-permute-start(f32[5,8,8,1]{3,2,0,1:T(8,128)S(1)} %get-tuple-element.35), channel_id=1, source_target_pairs={{0,8},{8,16},{16,24},{24,0},{1,9},{9,17},{17,25},{25,1},{2,10},{10... | collective-permute-start | bytes 3848 | tf_op jit(solution)/shard_map/ppermute | solution.py:28
  12.3 2.2 %collective-permute-start = (f32[5,8,8,1]{3,2,0,1:T(8,128)S(1)}, f32[5,8,8,1]{3,2,0,1:T(8,128)S(1)}, u32[]{:S(2)}, u32[]{:S(2)}) collective-permute-start(f32[5,8,8,1]{3,2,0,1:T(8,128)S(1)} %get-tuple-element.36), channel_id=1, source_target_pairs={{8,0},{16,8},{24,16},{0,24},{9,1},{17,9},{25,17},{1,25},{10,2},{18... | collective-permute-start | bytes 3848 | tf_op jit(solution)/shard_map/ppermute | solution.py:29
  26.8 5.3 %collective-permute-done.9 = f32[5,8,128]{2,1,0:T(8,128)S(1)} collective-permute-done((f32[5,8,128]{2,1,0:T(8,128)S(1)}, f32[5,8,128]{2,1,0:T(8,128)S(1)}, u32[]{:S(2)}, u32[]{:S(2)}) %collective-permute-start.9) | collective-permute-done | bytes 20512 | tf_op jit(solution)/shard_map/ppermute | solution.py:12
  32.5 1.3 %collective-permute-start.12 = (f32[5,8,1,128]{3,2,0,1:T(1,128)S(1)}, f32[5,8,1,128]{3,2,0,1:T(1,128)S(1)}, u32[]{:S(2)}, u32[]{:S(2)}) collective-permute-start(f32[5,8,1,128]{3,2,0,1:T(1,128)S(1)} %get-tuple-element.31), channel_id=1, source_target_pairs={{2,0},{4,2},{6,4},{3,1},{5,3},{7,5},{10,8},{12,10},{14,12},{11,9},... | collective-permute-start | bytes 61448 | tf_op jit(solution)/shard_map/ppermute | solution.py:29
  33.8 5.2 %collective-permute-start.13 = (f32[5,8,1,128]{3,2,0,1:T(1,128)S(1)}, f32[5,8,1,128]{3,2,0,1:T(1,128)S(1)}, u32[]{:S(2)}, u32[]{:S(2)}) collective-permute-start(f32[5,8,1,128]{3,2,0,1:T(1,128)S(1)} %get-tuple-element.32), channel_id=1, source_target_pairs={{0,2},{2,4},{4,6},{1,3},{3,5},{5,7},{8,10},{10,12},{12,14},{9,11},... | collective-permute-start | bytes 61448 | tf_op jit(solution)/shard_map/ppermute | solution.py:28
  39.1 3.8 %collective-permute-start.7 = (f32[5,8,8,1]{3,2,0,1:T(8,128)S(1)}, f32[5,8,8,1]{3,2,0,1:T(8,128)S(1)}, u32[]{:S(2)}, u32[]{:S(2)}) collective-permute-start(f32[5,8,8,1]{3,2,0,1:T(8,128)S(1)} %get-tuple-element.28), channel_id=1, source_target_pairs={{8,0},{16,8},{24,16},{0,24},{9,1},{17,9},{25,17},{1,25},{10,2},{18... | collective-permute-start | bytes 3848 | tf_op jit(solution)/shard_map/ppermute | solution.py:29
  43.0 4.4 %collective-permute-done.8 = f32[5,8,8,1]{3,2,0,1:T(8,128)S(1)} collective-permute-done((f32[5,8,8,1]{3,2,0,1:T(8,128)S(1)}, f32[5,8,8,1]{3,2,0,1:T(8,128)S(1)}, u32[]{:S(2)}, u32[]{:S(2)}) %collective-permute-start.8) | collective-permute-done | bytes 1312 | tf_op jit(solution)/shard_map/ppermute | solution.py:28
  49.2 1.3 %collective-permute-start.16 = (f32[5,8,128]{2,1,0:T(8,128)S(1)}, f32[5,8,128]{2,1,0:T(8,128)S(1)}, u32[]{:S(2)}, u32[]{:S(2)}) collective-permute-start(f32[5,8,128]{2,1,0:T(8,128)S(1)} %fusion.17), channel_id=1, source_target_pairs={{0,8},{8,16},{16,24},{24,0},{1,9},{9,17},{17,25},{25,1},{2,10},{10... | collective-permute-start | bytes 61448 | tf_op jit(solution)/shard_map/ppermute | solution.py:12
  50.5 4.3 %collective-permute-done.16 = f32[5,8,128]{2,1,0:T(8,128)S(1)} collective-permute-done((f32[5,8,128]{2,1,0:T(8,128)S(1)}, f32[5,8,128]{2,1,0:T(8,128)S(1)}, u32[]{:S(2)}, u32[]{:S(2)}) %collective-permute-start.16) | collective-permute-done | bytes 20512 | tf_op jit(solution)/shard_map/ppermute | solution.py:12
  55.0 1.3 %collective-permute-start.19 = (f32[5,8,1,128]{3,2,0,1:T(1,128)S(1)}, f32[5,8,1,128]{3,2,0,1:T(1,128)S(1)}, u32[]{:S(2)}, u32[]{:S(2)}) collective-permute-start(f32[5,8,1,128]{3,2,0,1:T(1,128)S(1)} %get-tuple-element.23), channel_id=1, source_target_pairs={{2,0},{4,2},{6,4},{3,1},{5,3},{7,5},{10,8},{12,10},{14,12},{11,9},... | collective-permute-start | bytes 61448 | tf_op jit(solution)/shard_map/ppermute | solution.py:29
  56.3 5.3 %collective-permute-start.20 = (f32[5,8,1,128]{3,2,0,1:T(1,128)S(1)}, f32[5,8,1,128]{3,2,0,1:T(1,128)S(1)}, u32[]{:S(2)}, u32[]{:S(2)}) collective-permute-start(f32[5,8,1,128]{3,2,0,1:T(1,128)S(1)} %get-tuple-element.24), channel_id=1, source_target_pairs={{0,2},{2,4},{4,6},{1,3},{3,5},{5,7},{8,10},{10,12},{12,14},{9,11},... | collective-permute-start | bytes 61448 | tf_op jit(solution)/shard_map/ppermute | solution.py:28
  62.3 3.2 %collective-permute-start.14 = (f32[5,8,8,1]{3,2,0,1:T(8,128)S(1)}, f32[5,8,8,1]{3,2,0,1:T(8,128)S(1)}, u32[]{:S(2)}, u32[]{:S(2)}) collective-permute-start(f32[5,8,8,1]{3,2,0,1:T(8,128)S(1)} %get-tuple-element.20), channel_id=1, source_target_pairs={{8,0},{16,8},{24,16},{0,24},{9,1},{17,9},{25,17},{1,25},{10,2},{18... | collective-permute-start | bytes 3848 | tf_op jit(solution)/shard_map/ppermute | solution.py:29
  65.5 3.4 %collective-permute-done.15 = f32[5,8,8,1]{3,2,0,1:T(8,128)S(1)} collective-permute-done((f32[5,8,8,1]{3,2,0,1:T(8,128)S(1)}, f32[5,8,8,1]{3,2,0,1:T(8,128)S(1)}, u32[]{:S(2)}, u32[]{:S(2)}) %collective-permute-start.15) | collective-permute-done | bytes 1312 | tf_op jit(solution)/shard_map/ppermute | solution.py:28
  68.9 1.2 %collective-permute-done.14 = f32[5,8,8,1]{3,2,0,1:T(8,128)S(1)} collective-permute-done((f32[5,8,8,1]{3,2,0,1:T(8,128)S(1)}, f32[5,8,8,1]{3,2,0,1:T(8,128)S(1)}, u32[]{:S(2)}, u32[]{:S(2)}) %collective-permute-start.14) | collective-permute-done | bytes 1312 | tf_op jit(solution)/shard_map/ppermute | solution.py:29
  72.1 4.6 %collective-permute-done.23 = f32[5,8,128]{2,1,0:T(8,128)S(1)} collective-permute-done((f32[5,8,128]{2,1,0:T(8,128)S(1)}, f32[5,8,128]{2,1,0:T(8,128)S(1)}, u32[]{:S(2)}, u32[]{:S(2)}) %collective-permute-start.23) | collective-permute-done | bytes 20512 | tf_op jit(solution)/shard_map/ppermute | solution.py:12
  76.8 4.8 %collective-permute-start.27 = (f32[5,8,1,128]{3,2,0,1:T(1,128)S(1)}, f32[5,8,1,128]{3,2,0,1:T(1,128)S(1)}, u32[]{:S(2)}, u32[]{:S(2)}) collective-permute-start(f32[5,8,1,128]{3,2,0,1:T(1,128)S(1)} %get-tuple-element.13), channel_id=1, source_target_pairs={{0,2},{2,4},{4,6},{1,3},{3,5},{5,7},{8,10},{10,12},{12,14},{9,11},... | collective-permute-start | bytes 61448 | tf_op jit(solution)/shard_map/ppermute | solution.py:28
  81.6 1.3 %collective-permute-start.26 = (f32[5,8,1,128]{3,2,0,1:T(1,128)S(1)}, f32[5,8,1,128]{3,2,0,1:T(1,128)S(1)}, u32[]{:S(2)}, u32[]{:S(2)}) collective-permute-start(f32[5,8,1,128]{3,2,0,1:T(1,128)S(1)} %get-tuple-element.14), channel_id=1, source_target_pairs={{2,0},{4,2},{6,4},{3,1},{5,3},{7,5},{10,8},{12,10},{14,12},{11,9},... | collective-permute-start | bytes 61448 | tf_op jit(solution)/shard_map/ppermute | solution.py:29
  82.9 1.4 %collective-permute-start.22 = (f32[5,8,8,1]{3,2,0,1:T(8,128)S(1)}, f32[5,8,8,1]{3,2,0,1:T(8,128)S(1)}, u32[]{:S(2)}, u32[]{:S(2)}) collective-permute-start(f32[5,8,8,1]{3,2,0,1:T(8,128)S(1)} %get-tuple-element.11), channel_id=1, source_target_pairs={{0,8},{8,16},{16,24},{24,0},{1,9},{9,17},{17,25},{25,1},{2,10},{10... | collective-permute-start | bytes 3848 | tf_op jit(solution)/shard_map/ppermute | solution.py:28
  84.3 2.5 %collective-permute-start.21 = (f32[5,8,8,1]{3,2,0,1:T(8,128)S(1)}, f32[5,8,8,1]{3,2,0,1:T(8,128)S(1)}, u32[]{:S(2)}, u32[]{:S(2)}) collective-permute-start(f32[5,8,8,1]{3,2,0,1:T(8,128)S(1)} %get-tuple-element.12), channel_id=1, source_target_pairs={{8,0},{16,8},{24,16},{0,24},{9,1},{17,9},{25,17},{1,25},{10,2},{18... | collective-permute-start | bytes 3848 | tf_op jit(solution)/shard_map/ppermute | solution.py:29
  86.9 3.4 %collective-permute-done.22 = f32[5,8,8,1]{3,2,0,1:T(8,128)S(1)} collective-permute-done((f32[5,8,8,1]{3,2,0,1:T(8,128)S(1)}, f32[5,8,8,1]{3,2,0,1:T(8,128)S(1)}, u32[]{:S(2)}, u32[]{:S(2)}) %collective-permute-start.22) | collective-permute-done | bytes 1312 | tf_op jit(solution)/shard_map/ppermute | solution.py:28
  90.3 1.2 %collective-permute-done.21 = f32[5,8,8,1]{3,2,0,1:T(8,128)S(1)} collective-permute-done((f32[5,8,8,1]{3,2,0,1:T(8,128)S(1)}, f32[5,8,8,1]{3,2,0,1:T(8,128)S(1)}, u32[]{:S(2)}, u32[]{:S(2)}) %collective-permute-start.21) | collective-permute-done | bytes 1312 | tf_op jit(solution)/shard_map/ppermute | solution.py:29
  (123 shorter events, 16.6 us)
Async XLA Ops:
  0.8 17.8 %collective-permute-start.2 = (f32[5,8,128]{2,1,0:T(8,128)S(1)}, f32[5,8,128]{2,1,0:T(8,128)S(1)}, u32[]{:S(2)}, u32[]{:S(2)}) collective-permute-start(f32[5,8,128]{2,1,0:T(8,128)S(1)} %fusion.19), channel_id=1, source_target_pairs={{0,8},{8,16},{16,24},{24,0},{1,9},{9,17},{17,25},{25,1},{2,10},{10... | collective-permute-start | bytes 61448 | tf_op jit(solution)/shard_map/ppermute | solution.py:12
  4.8 19.1 %collective-permute-start.6 = (f32[5,8,1,128]{3,2,0,1:T(1,128)S(1)}, f32[5,8,1,128]{3,2,0,1:T(1,128)S(1)}, u32[]{:S(2)}, u32[]{:S(2)}) collective-permute-start(f32[5,8,1,128]{3,2,0,1:T(1,128)S(1)} %get-tuple-element.39), channel_id=1, source_target_pairs={{0,2},{2,4},{4,6},{1,3},{3,5},{5,7},{8,10},{10,12},{12,14},{9,11},... | collective-permute-start | bytes 61448 | tf_op jit(solution)/shard_map/ppermute | solution.py:28
  8.2 15.7 %collective-permute-start.5 = (f32[5,8,1,128]{3,2,0,1:T(1,128)S(1)}, f32[5,8,1,128]{3,2,0,1:T(1,128)S(1)}, u32[]{:S(2)}, u32[]{:S(2)}) collective-permute-start(f32[5,8,1,128]{3,2,0,1:T(1,128)S(1)} %get-tuple-element.40), channel_id=1, source_target_pairs={{2,0},{4,2},{6,4},{3,1},{5,3},{7,5},{10,8},{12,10},{14,12},{11,9},... | collective-permute-start | bytes 61448 | tf_op jit(solution)/shard_map/ppermute | solution.py:29
  10.7 13.2 %collective-permute-start.1 = (f32[5,8,8,1]{3,2,0,1:T(8,128)S(1)}, f32[5,8,8,1]{3,2,0,1:T(8,128)S(1)}, u32[]{:S(2)}, u32[]{:S(2)}) collective-permute-start(f32[5,8,8,1]{3,2,0,1:T(8,128)S(1)} %get-tuple-element.35), channel_id=1, source_target_pairs={{0,8},{8,16},{16,24},{24,0},{1,9},{9,17},{17,25},{25,1},{2,10},{10... | collective-permute-start | bytes 3848 | tf_op jit(solution)/shard_map/ppermute | solution.py:28
  12.3 11.6 %collective-permute-start = (f32[5,8,8,1]{3,2,0,1:T(8,128)S(1)}, f32[5,8,8,1]{3,2,0,1:T(8,128)S(1)}, u32[]{:S(2)}, u32[]{:S(2)}) collective-permute-start(f32[5,8,8,1]{3,2,0,1:T(8,128)S(1)} %get-tuple-element.36), channel_id=1, source_target_pairs={{8,0},{16,8},{24,16},{0,24},{9,1},{17,9},{25,17},{1,25},{10,2},{18... | collective-permute-start | bytes 3848 | tf_op jit(solution)/shard_map/ppermute | solution.py:29
  26.5 5.6 %collective-permute-start.9 = (f32[5,8,128]{2,1,0:T(8,128)S(1)}, f32[5,8,128]{2,1,0:T(8,128)S(1)}, u32[]{:S(2)}, u32[]{:S(2)}) collective-permute-start(f32[5,8,128]{2,1,0:T(8,128)S(1)} %fusion.18), channel_id=1, source_target_pairs={{0,8},{8,16},{16,24},{24,0},{1,9},{9,17},{17,25},{25,1},{2,10},{10... | collective-permute-start | bytes 61448 | tf_op jit(solution)/shard_map/ppermute | solution.py:12
  32.1 10.7 %collective-permute-start.10 = (f32[5,8,128]{2,1,0:T(8,128)S(1)}, f32[5,8,128]{2,1,0:T(8,128)S(1)}, u32[]{:S(2)}, u32[]{:S(2)}) collective-permute-start(f32[5,8,128]{2,1,0:T(8,128)S(1)} %broadcast_select_fusion.4), channel_id=1, source_target_pairs={{0,16},{8,24},{16,0},{24,8},{1,17},{9,25},{17,1},{25,9},{2,18},{10... | collective-permute-start | bytes 61448 | tf_op jit(solution)/shard_map/ppermute | solution.py:12
  32.5 15.7 %collective-permute-start.12 = (f32[5,8,1,128]{3,2,0,1:T(1,128)S(1)}, f32[5,8,1,128]{3,2,0,1:T(1,128)S(1)}, u32[]{:S(2)}, u32[]{:S(2)}) collective-permute-start(f32[5,8,1,128]{3,2,0,1:T(1,128)S(1)} %get-tuple-element.31), channel_id=1, source_target_pairs={{2,0},{4,2},{6,4},{3,1},{5,3},{7,5},{10,8},{12,10},{14,12},{11,9},... | collective-permute-start | bytes 61448 | tf_op jit(solution)/shard_map/ppermute | solution.py:29
  33.8 14.4 %collective-permute-start.13 = (f32[5,8,1,128]{3,2,0,1:T(1,128)S(1)}, f32[5,8,1,128]{3,2,0,1:T(1,128)S(1)}, u32[]{:S(2)}, u32[]{:S(2)}) collective-permute-start(f32[5,8,1,128]{3,2,0,1:T(1,128)S(1)} %get-tuple-element.32), channel_id=1, source_target_pairs={{0,2},{2,4},{4,6},{1,3},{3,5},{5,7},{8,10},{10,12},{12,14},{9,11},... | collective-permute-start | bytes 61448 | tf_op jit(solution)/shard_map/ppermute | solution.py:28
  39.0 8.3 %collective-permute-start.8 = (f32[5,8,8,1]{3,2,0,1:T(8,128)S(1)}, f32[5,8,8,1]{3,2,0,1:T(8,128)S(1)}, u32[]{:S(2)}, u32[]{:S(2)}) collective-permute-start(f32[5,8,8,1]{3,2,0,1:T(8,128)S(1)} %get-tuple-element.27), channel_id=1, source_target_pairs={{0,8},{8,16},{16,24},{24,0},{1,9},{9,17},{17,25},{25,1},{2,10},{10... | collective-permute-start | bytes 3848 | tf_op jit(solution)/shard_map/ppermute | solution.py:28
  39.1 9.2 %collective-permute-start.7 = (f32[5,8,8,1]{3,2,0,1:T(8,128)S(1)}, f32[5,8,8,1]{3,2,0,1:T(8,128)S(1)}, u32[]{:S(2)}, u32[]{:S(2)}) collective-permute-start(f32[5,8,8,1]{3,2,0,1:T(8,128)S(1)} %get-tuple-element.28), channel_id=1, source_target_pairs={{8,0},{16,8},{24,16},{0,24},{9,1},{17,9},{25,17},{1,25},{10,2},{18... | collective-permute-start | bytes 3848 | tf_op jit(solution)/shard_map/ppermute | solution.py:29
  42.9 5.6 %collective-permute-start.11 = (f32[5,8,128]{2,1,0:T(8,128)S(1)}, f32[5,8,128]{2,1,0:T(8,128)S(1)}, u32[]{:S(2)}, u32[]{:S(2)}) collective-permute-start(f32[5,8,128]{2,1,0:T(8,128)S(1)} %broadcast_select_fusion.5), channel_id=1, source_target_pairs={{0,1},{1,0},{2,3},{3,2},{4,5},{5,4},{6,7},{7,6},{8,9},{9,8},{10,11... | collective-permute-start | bytes 61448 | tf_op jit(solution)/shard_map/ppermute | solution.py:18
  49.2 5.6 %collective-permute-start.16 = (f32[5,8,128]{2,1,0:T(8,128)S(1)}, f32[5,8,128]{2,1,0:T(8,128)S(1)}, u32[]{:S(2)}, u32[]{:S(2)}) collective-permute-start(f32[5,8,128]{2,1,0:T(8,128)S(1)} %fusion.17), channel_id=1, source_target_pairs={{0,8},{8,16},{16,24},{24,0},{1,9},{9,17},{17,25},{25,1},{2,10},{10... | collective-permute-start | bytes 61448 | tf_op jit(solution)/shard_map/ppermute | solution.py:12
  54.9 10.6 %collective-permute-start.17 = (f32[5,8,128]{2,1,0:T(8,128)S(1)}, f32[5,8,128]{2,1,0:T(8,128)S(1)}, u32[]{:S(2)}, u32[]{:S(2)}) collective-permute-start(f32[5,8,128]{2,1,0:T(8,128)S(1)} %broadcast_select_fusion.2), channel_id=1, source_target_pairs={{0,16},{8,24},{16,0},{24,8},{1,17},{9,25},{17,1},{25,9},{2,18},{10... | collective-permute-start | bytes 61448 | tf_op jit(solution)/shard_map/ppermute | solution.py:12
  55.0 15.2 %collective-permute-start.19 = (f32[5,8,1,128]{3,2,0,1:T(1,128)S(1)}, f32[5,8,1,128]{3,2,0,1:T(1,128)S(1)}, u32[]{:S(2)}, u32[]{:S(2)}) collective-permute-start(f32[5,8,1,128]{3,2,0,1:T(1,128)S(1)} %get-tuple-element.23), channel_id=1, source_target_pairs={{2,0},{4,2},{6,4},{3,1},{5,3},{7,5},{10,8},{12,10},{14,12},{11,9},... | collective-permute-start | bytes 61448 | tf_op jit(solution)/shard_map/ppermute | solution.py:29
  56.3 13.9 %collective-permute-start.20 = (f32[5,8,1,128]{3,2,0,1:T(1,128)S(1)}, f32[5,8,1,128]{3,2,0,1:T(1,128)S(1)}, u32[]{:S(2)}, u32[]{:S(2)}) collective-permute-start(f32[5,8,1,128]{3,2,0,1:T(1,128)S(1)} %get-tuple-element.24), channel_id=1, source_target_pairs={{0,2},{2,4},{4,6},{1,3},{3,5},{5,7},{8,10},{10,12},{12,14},{9,11},... | collective-permute-start | bytes 61448 | tf_op jit(solution)/shard_map/ppermute | solution.py:28
  61.6 7.3 %collective-permute-start.15 = (f32[5,8,8,1]{3,2,0,1:T(8,128)S(1)}, f32[5,8,8,1]{3,2,0,1:T(8,128)S(1)}, u32[]{:S(2)}, u32[]{:S(2)}) collective-permute-start(f32[5,8,8,1]{3,2,0,1:T(8,128)S(1)} %get-tuple-element.19), channel_id=1, source_target_pairs={{0,8},{8,16},{16,24},{24,0},{1,9},{9,17},{17,25},{25,1},{2,10},{10... | collective-permute-start | bytes 3848 | tf_op jit(solution)/shard_map/ppermute | solution.py:28
  62.3 7.9 %collective-permute-start.14 = (f32[5,8,8,1]{3,2,0,1:T(8,128)S(1)}, f32[5,8,8,1]{3,2,0,1:T(8,128)S(1)}, u32[]{:S(2)}, u32[]{:S(2)}) collective-permute-start(f32[5,8,8,1]{3,2,0,1:T(8,128)S(1)} %get-tuple-element.20), channel_id=1, source_target_pairs={{8,0},{16,8},{24,16},{0,24},{9,1},{17,9},{25,17},{1,25},{10,2},{18... | collective-permute-start | bytes 3848 | tf_op jit(solution)/shard_map/ppermute | solution.py:29
  71.1 5.6 %collective-permute-start.23 = (f32[5,8,128]{2,1,0:T(8,128)S(1)}, f32[5,8,128]{2,1,0:T(8,128)S(1)}, u32[]{:S(2)}, u32[]{:S(2)}) collective-permute-start(f32[5,8,128]{2,1,0:T(8,128)S(1)} %fusion.16), channel_id=1, source_target_pairs={{0,8},{8,16},{16,24},{24,0},{1,9},{9,17},{17,25},{25,1},{2,10},{10... | collective-permute-start | bytes 61448 | tf_op jit(solution)/shard_map/ppermute | solution.py:12
  76.8 10.1 %collective-permute-start.24 = (f32[5,8,128]{2,1,0:T(8,128)S(1)}, f32[5,8,128]{2,1,0:T(8,128)S(1)}, u32[]{:S(2)}, u32[]{:S(2)}) collective-permute-start(f32[5,8,128]{2,1,0:T(8,128)S(1)} %broadcast_select_fusion), channel_id=1, source_target_pairs={{0,16},{8,24},{16,0},{24,8},{1,17},{9,25},{17,1},{25,9},{2,18},{10... | collective-permute-start | bytes 61448 | tf_op jit(solution)/shard_map/ppermute | solution.py:12
  76.8 14.7 %collective-permute-start.27 = (f32[5,8,1,128]{3,2,0,1:T(1,128)S(1)}, f32[5,8,1,128]{3,2,0,1:T(1,128)S(1)}, u32[]{:S(2)}, u32[]{:S(2)}) collective-permute-start(f32[5,8,1,128]{3,2,0,1:T(1,128)S(1)} %get-tuple-element.13), channel_id=1, source_target_pairs={{0,2},{2,4},{4,6},{1,3},{3,5},{5,7},{8,10},{10,12},{12,14},{9,11},... | collective-permute-start | bytes 61448 | tf_op jit(solution)/shard_map/ppermute | solution.py:28
  81.6 9.9 %collective-permute-start.26 = (f32[5,8,1,128]{3,2,0,1:T(1,128)S(1)}, f32[5,8,1,128]{3,2,0,1:T(1,128)S(1)}, u32[]{:S(2)}, u32[]{:S(2)}) collective-permute-start(f32[5,8,1,128]{3,2,0,1:T(1,128)S(1)} %get-tuple-element.14), channel_id=1, source_target_pairs={{2,0},{4,2},{6,4},{3,1},{5,3},{7,5},{10,8},{12,10},{14,12},{11,9},... | collective-permute-start | bytes 61448 | tf_op jit(solution)/shard_map/ppermute | solution.py:29
  82.9 7.3 %collective-permute-start.22 = (f32[5,8,8,1]{3,2,0,1:T(8,128)S(1)}, f32[5,8,8,1]{3,2,0,1:T(8,128)S(1)}, u32[]{:S(2)}, u32[]{:S(2)}) collective-permute-start(f32[5,8,8,1]{3,2,0,1:T(8,128)S(1)} %get-tuple-element.11), channel_id=1, source_target_pairs={{0,8},{8,16},{16,24},{24,0},{1,9},{9,17},{17,25},{25,1},{2,10},{10... | collective-permute-start | bytes 3848 | tf_op jit(solution)/shard_map/ppermute | solution.py:28
  84.3 7.2 %collective-permute-start.21 = (f32[5,8,8,1]{3,2,0,1:T(8,128)S(1)}, f32[5,8,8,1]{3,2,0,1:T(8,128)S(1)}, u32[]{:S(2)}, u32[]{:S(2)}) collective-permute-start(f32[5,8,8,1]{3,2,0,1:T(8,128)S(1)} %get-tuple-element.12), channel_id=1, source_target_pairs={{8,0},{16,8},{24,16},{0,24},{9,1},{17,9},{25,17},{1,25},{10,2},{18... | collective-permute-start | bytes 3848 | tf_op jit(solution)/shard_map/ppermute | solution.py:29
  (9 other events, 24.8 us)
where the time goes:
time: 93.9 us; the launch traced here: 93.3 us
  starting transfers between devices  46.5 us (50%)
  waiting for transfers between devices  29.7 us (32%)
  local copies, waits for them, and re-layouts  6.14 us (7%)
  between operations  5.9 us (6%)
  other arithmetic  4.01 us (4%)
  matrix products  0.97 us (1%)
    ppermute x8, starting transfers between devices, padded(): before = lax.ppermute(last, axis, up)  22.4 us
    ppermute x8, starting transfers between devices, padded(): after = lax.ppermute(leading, axis, down)  16.9 us
    ppermute x8, waiting for transfers between devices, passed_along(): return lax.ppermute(x, axis, [(i, (i + by) % count) for i in range(count)])  14.3 us
    ppermute x8, waiting for transfers between devices, padded(): before = lax.ppermute(last, axis, up)  11.1 us
    ppermute x8, starting transfers between devices, passed_along(): return lax.ppermute(x, axis, [(i, (i + by) % count) for i in range(count)])  6.89 us
    ppermute x8, waiting for transfers between devices, padded(): after = lax.ppermute(leading, axis, down)  3.42 us
    slice x6, local copies, waits for them, and re-layouts, padded(): last = lax.slice_in_dim(x, length - width, length, axis=dim)  2.5 us
    unnamed x23, local copies, waits for them, and re-layouts  2.13 us
  transfers between devices with their start and end apart: 28, of which 10 were waited for; matrix products, arithmetic and copies ran while one was open for 5% of the time, Pallas kernels for 0%

commit v1 on v0

v1 whole, which is shorter than its diff:
```python
import functools

import jax
import jax.numpy as jnp
from jax import lax
from jax.experimental import pallas as pl
from jax.experimental.pallas import tpu as pltpu
from jax.sharding import PartitionSpec as P

AXIAL_MACH = 0.4
STEP_SIZE = 0.3
MESH = pl.DeviceIdType.MESH
STAGE = (0.5 * STEP_SIZE, 0.5 * STEP_SIZE, STEP_SIZE)
BLEND = (1.0, 2.0, 2.0, 1.0)


def build_table(index, weight):
    taps, width = index.shape
    normed = weight / jnp.sum(weight, axis=0, keepdims=True)
    source = lax.broadcasted_iota(jnp.int32, (width, width), 0)
    matrix = jnp.zeros((width, width), jnp.float32)
    for tap in range(taps):
        matrix += jnp.where(index[tap : tap + 1] == source, normed[tap : tap + 1], 0.0)
    high = matrix.astype(jnp.bfloat16)
    low = (matrix - high.astype(jnp.float32)).astype(jnp.bfloat16)
    top = jnp.concatenate([high, low], axis=1)
    bottom = jnp.concatenate([high, jnp.zeros_like(high)], axis=1)
    return jnp.concatenate([top, bottom], axis=0)


def interpolate(plane, table):
    width = plane.shape[1]
    high = plane.astype(jnp.bfloat16)
    low = (plane - high.astype(jnp.float32)).astype(jnp.bfloat16)
    both = jnp.dot(
        jnp.concatenate([high, low], axis=1), table, preferred_element_type=jnp.float32
    )
    return both[:, :width] + both[:, width:]


def kernel(
    n_circ, n_rad,
    state_ref, eddy_ref, offset_ref, index_ref, weight_ref, out_ref,
    field, total, table, plane_out, rad_out, rad_in, circ_out, circ_in,
    plane_send, plane_recv, rad_send, rad_recv, circ_send, circ_recv, *plane_in,
):
    nvar, naxial, nradial, width = state_ref.shape
    sections = offset_ref.shape[0]
    rows = nvar * nradial
    tiles = nvar * naxial
    circ, rad, ax = lax.axis_index("circ"), lax.axis_index("rad"), lax.axis_index("ax")
    far = 1 - ax
    circ_up, circ_down = lax.rem(circ + 1, n_circ), lax.rem(circ + n_circ - 1, n_circ)
    has_low, has_high = rad > 0, rad < n_rad - 1
    front = jnp.where(ax == 0, naxial - 1, 0)
    front_rows = pl.ds(pl.multiple_of(front * rows, 8), rows)

    barrier = pltpu.get_barrier_semaphore()

    def greet(device):
        pl.semaphore_signal(barrier, inc=1, device_id=device, device_id_type=MESH)

    for apart in range(n_circ):
        greet((lax.rem(circ + apart, n_circ), rad, far))
    greet((circ_up, rad, ax))
    greet((circ_down, rad, ax))

    @pl.when(has_low)
    def _():
        greet((circ, rad - 1, ax))

    @pl.when(has_high)
    def _():
        greet((circ, rad + 1, ax))

    for a in range(naxial):
        field[0, a * rows : (a + 1) * rows, :] = state_ref[:, a].reshape(rows, width)

    @pl.when(jnp.logical_not(has_low))
    def _():
        for s in range(sections):
            rad_in[s, 0] = jnp.zeros((tiles, width), jnp.float32)

    @pl.when(jnp.logical_not(has_high))
    def _():
        for s in range(sections):
            rad_in[s, 1] = jnp.zeros((tiles, width), jnp.float32)

    pl.semaphore_wait(
        barrier, n_circ + 2 + jnp.where(has_low, 1, 0) + jnp.where(has_high, 1, 0)
    )

    def plane_copy(s, apart):
        return pltpu.make_async_remote_copy(
            src_ref=plane_out.at[s], dst_ref=plane_in[s].at[circ],
            send_sem=plane_send.at[s, apart], recv_sem=plane_recv.at[s, circ],
            device_id=(lax.rem(circ + apart, n_circ), rad, far), device_id_type=MESH,
        )

    def plane_arrival(s, source):
        return pltpu.make_async_remote_copy(
            src_ref=plane_out.at[s], dst_ref=plane_in[s].at[source],
            send_sem=plane_send.at[s, 0], recv_sem=plane_recv.at[s, source],
            device_id=(source, rad, far), device_id_type=MESH,
        )

    def circ_copy(s, side):
        return pltpu.make_async_remote_copy(
            src_ref=circ_out.at[s, side], dst_ref=circ_in.at[s, side],
            send_sem=circ_send.at[s, side], recv_sem=circ_recv.at[s, side],
            device_id=(circ_up if side == 0 else circ_down, rad, ax), device_id_type=MESH,
        )

    def rad_copy(s, side):
        return pltpu.make_async_remote_copy(
            src_ref=rad_out.at[s, side], dst_ref=rad_in.at[s, side],
            send_sem=rad_send.at[s, side], recv_sem=rad_recv.at[s, side],
            device_id=(circ, rad + 1 if side == 0 else rad - 1, ax), device_id_type=MESH,
        )

    sends_rad = (has_high, has_low)
    gets_rad = (has_low, has_high)
    lane = lax.broadcasted_iota(jnp.int32, (nvar, nradial, width), 2)
    sub = lax.broadcasted_iota(jnp.int32, (nvar, nradial, width), 1)
    swirl = jnp.where(ax == 1, -0.3, 0.2).astype(jnp.float32)
    toward = jnp.where(ax == 1, -0.5, 0.5).astype(jnp.float32)
    wide = lax.broadcasted_iota(jnp.int32, (tiles, nradial, width), 2)
    tile_of = lax.broadcasted_iota(jnp.int32, (tiles, nradial, width), 0)

    for s in range(sections):
        last = s == sections - 1
        plane_out[s] = field[s, front_rows, :]
        for apart in reversed(range(n_circ)):
            plane_copy(s, apart).start()

        cells = field[s].reshape(tiles, nradial, width)
        for side, edge in ((0, width - 1), (1, 0)):
            column = jnp.broadcast_to(cells[:, :, edge : edge + 1], cells.shape)
            circ_out[s, side] = jnp.sum(jnp.where(wide == tile_of, column, 0.0), axis=0)
            circ_copy(s, side).start()
        for side, edge in ((0, nradial - 1), (1, 0)):
            rad_out[s, side] = field[s, pl.ds(edge, tiles, stride=nradial), :]

            @pl.when(sends_rad[side])
            def _():
                rad_copy(s, side).start()

        table[s] = build_table(index_ref[ax, s], weight_ref[ax, s])

        for side in range(2):
            circ_copy(s, side).wait_recv()

            @pl.when(gets_rad[side])
            def _():
                rad_copy(s, side).wait_recv()

        circ_low_edge, circ_high_edge = circ_in[s, 0], circ_in[s, 1]

        def spread(edges, a):
            picked = [
                jnp.broadcast_to(edges[:, t : t + 1], (nradial, width))
                for t in range(a * nvar, (a + 1) * nvar)
            ]
            return jnp.stack(picked)

        def spread_rows(side, a):
            picked = rad_in[s, side, a * nvar : (a + 1) * nvar, :]
            return jnp.broadcast_to(picked[:, None, :], (nvar, nradial, width))

        def plane_at(a):
            return field[s, a * rows : (a + 1) * rows, :].reshape(nvar, nradial, width)

        zero = jnp.zeros((nvar, nradial, width), jnp.float32)
        for a in range(naxial):
            q = plane_at(a)
            axial_low = plane_at(a - 1) if a > 0 else zero
            axial_high = plane_at(a + 1) if a < naxial - 1 else zero
            circ_low = jnp.where(lane == 0, spread(circ_low_edge, a), pltpu.roll(q, 1, 2))
            circ_high = jnp.where(
                lane == width - 1, spread(circ_high_edge, a), pltpu.roll(q, width - 1, 2)
            )
            rad_low = jnp.where(sub == 0, spread_rows(0, a), pltpu.roll(q, 1, 1))
            rad_high = jnp.where(
                sub == nradial - 1, spread_rows(1, a), pltpu.roll(q, nradial - 1, 1)
            )
            diff_circ = 0.5 * (circ_high - circ_low)
            diff_axial = 0.5 * (axial_high - axial_low)
            laplace = (
                (circ_high + circ_low) + (rad_high + rad_low) + (axial_high + axial_low) - 6.0 * q
            )
            slope = eddy_ref[a][None] * laplace - (swirl * diff_circ + AXIAL_MACH * diff_axial)
            diff_rad_2 = 0.5 * (rad_high[2] - rad_low[2])
            diff_rad_4 = 0.5 * (rad_high[4] - rad_low[4])
            diverge = diff_circ[1] + diff_rad_2 + diff_axial[3]
            flux = jnp.stack([diverge, diff_circ[4], diff_rad_4, diff_axial[4], diverge])
            slope = slope - flux
            base = state_ref[:, a]
            if s == 0:
                total[:, a] = slope
            else:
                total[:, a] += BLEND[s] * slope
            if not last:
                field[s + 1, a * rows : (a + 1) * rows, :] = (base + STAGE[s] * slope).reshape(
                    rows, width
                )

        for source in range(n_circ):
            plane_arrival(s, source).wait_recv()
        shift = jnp.where(ax == 1, offset_ref[s], n_circ - offset_ref[s])
        faced = plane_in[s][lax.rem(circ + shift, n_circ)]
        ghost = interpolate(faced, table[s]).reshape(nvar, nradial, width)
        slant = toward * ghost
        slope = eddy_ref[front][None] * ghost - AXIAL_MACH * slant
        none = jnp.zeros_like(slant[0])
        slope = slope - jnp.stack([slant[3], none, none, slant[4], slant[3]])
        total[:, front] += BLEND[s] * slope
        if not last:
            field[s + 1, front_rows, :] += (STAGE[s] * slope).reshape(rows, width)

    for a in range(naxial):
        out_ref[:, a] = state_ref[:, a] + (STEP_SIZE / 6.0) * total[:, a]

    for s in range(sections):
        for apart in range(n_circ):
            plane_copy(s, apart).wait_send()
        for side in range(2):
            circ_copy(s, side).wait_send()

            @pl.when(sends_rad[side])
            def _():
                rad_copy(s, side).wait_send()


def solution(mesh):
    n_circ, n_rad = mesh.shape["circ"], mesh.shape["rad"]

    def local(state, eddy, offsets, stencil_index, stencil_weight):
        nvar, naxial, nradial, width = state.shape
        sections = offsets.shape[0]
        rows, tiles = nvar * nradial, nvar * naxial
        vmem = pl.BlockSpec(memory_space=pltpu.VMEM)
        buffer = lambda *shape: pltpu.VMEM(shape, jnp.float32)
        return pl.pallas_call(
            functools.partial(kernel, n_circ, n_rad),
            out_shape=jax.ShapeDtypeStruct(state.shape, jnp.float32),
            in_specs=[vmem, vmem, pl.BlockSpec(memory_space=pltpu.SMEM), vmem, vmem],
            out_specs=vmem,
            scratch_shapes=[
                buffer(sections, rows * naxial, width),
                buffer(*state.shape),
                pltpu.VMEM((sections, 2 * width, 2 * width), jnp.bfloat16),
                buffer(sections, rows, width),
                buffer(sections, 2, tiles, width),
                buffer(sections, 2, tiles, width),
                buffer(sections, 2, nradial, width),
                buffer(sections, 2, nradial, width),
                pltpu.SemaphoreType.DMA((sections, n_circ)),
                pltpu.SemaphoreType.DMA((sections, n_circ)),
                pltpu.SemaphoreType.DMA((sections, 2)),
                pltpu.SemaphoreType.DMA((sections, 2)),
                pltpu.SemaphoreType.DMA((sections, 2)),
                pltpu.SemaphoreType.DMA((sections, 2)),
                *[buffer(n_circ, rows, width) for _ in range(sections)],
            ],
            compiler_params=pltpu.CompilerParams(
                collective_id=0, has_side_effects=True, vmem_limit_bytes=32 * 1024 * 1024
            ),
        )(state, eddy, offsets, jnp.swapaxes(stencil_index, 2, 3), jnp.swapaxes(stencil_weight, 2, 3))

    return jax.shard_map(
        local,
        mesh=mesh,
        in_specs=(P(None, "ax", "rad", "circ"), P("ax", "rad", "circ"), P(), P(), P()),
        out_specs=P(None, "ax", "rad", "circ"),
        check_vma=False,
    )
```

time: 93.9 us -> 29.9 us (0.32)
  starting transfers between devices: 46.5 us -> 0 us
  waiting for transfers between devices: 29.7 us -> 0 us
  Pallas kernels: 0 us -> 25.1 us
  between operations: 5.9 us -> 0.01 us
  other arithmetic: 4.01 us -> 0 us
  local copies, waits for them, and re-layouts: 6.14 us -> 4.43 us
  matrix products: 0.97 us -> 0 us
    ppermute x28 -> x0, starting transfers between devices: 46.5 us -> none  [the longest x8 22.4 us: padded(): before = lax.ppermute(last, axis, up)]
    ppermute x28 -> x0, waiting for transfers between devices: 29.7 us -> none  [the longest x8 14.3 us: passed_along(): return lax.ppermute(x, axis, [(i, (i + by) % count) for i in range(count)])]
    pallas_call x0 -> x1, Pallas kernels: none -> 25.1 us  [local(): pl.pallas_call(functools.partial(kernel, n_circ, n_rad), out_shape=jax.Sh...]
    slice x15 -> x0, local copies, waits for them, and re-layouts: 3.29 us -> none  [the longest x6 2.5 us: padded(): last = lax.slice_in_dim(x, length - width, length, axis=dim)]
    unnamed x23 -> x11, local copies, waits for them, and re-layouts: 2.13 us -> 4.43 us
    add x4 -> x0, other arithmetic: 1.28 us -> none  [the longest x1 0.51 us: local(): state + STEP_SIZE / 6.0 * (slope_one + 2.0 * slope_two + 2.0 * slope_thre...]
    dot_general x4 -> x0, matrix products: 0.97 us -> none  [facing_ghost(): jnp.dot(flat_rows, matrix.T, precision=lax.Precision.HIGHEST, preferred_e...]
  transfers between devices with their start and end apart: 28 -> 0, of which waited for: 10 -> 0; matrix products, arithmetic and copies ran while one was open for 5% -> 0% of each run, Pallas kernels for 0% -> 0%
where the time goes in v1:
time: 29.9 us; the launch traced here: 29.6 us
  Pallas kernels  25.1 us (84%)
  local copies, waits for them, and re-layouts  4.43 us (15%)
    pallas_call x1, Pallas kernels, local(): pl.pallas_call(functools.partial(kernel, n_circ, n_rad), out_shape=jax.Sh...  25.1 us
    unnamed x11, local copies, waits for them, and re-layouts  4.43 us

profile of v1, /device:TPU:0, one launch (start us, length us, event | category | flops | bytes accessed | tf_op | source)
XLA Modules:
  0.0 29.6 jit_solution(2104805496227220239)
XLA Ops:
  0.0 0.0 copy-start.4
  0.0 0.7 %copy-done.4 = s32[4]{0:T(128)S(1)} copy-done((s32[4]{0:T(128)S(1)}, s32[4]{0:T(128)}, u32[]{:S(2)}) %copy-start.4) | copy-done | bytes 40
  0.7 0.0 copy-start
  0.7 0.9 %copy-done = f32[5,8,8,128]{3,2,1,0:T(8,128)S(1)} copy-done((f32[5,8,8,128]{3,2,1,0:T(8,128)S(1)}, f32[5,8,8,128]{3,2,1,0:T(8,128)}, u32[]{:S(2)}) %copy-start) | copy-done | bytes 163864
  1.6 0.0 copy-start.1
  1.6 0.8 %copy-done.1 = f32[8,8,128]{2,1,0:T(8,128)S(1)} copy-done((f32[8,8,128]{2,1,0:T(8,128)S(1)}, f32[8,8,128]{2,1,0:T(8,128)}, u32[]{:S(2)}) %copy-start.1) | copy-done | bytes 32792
  2.3 0.0 copy-start.2
  2.3 0.7 %copy-done.2 = s32[2,4,128,4]{2,3,1,0:T(4,128)S(1)} copy-done((s32[2,4,128,4]{2,3,1,0:T(4,128)S(1)}, s32[2,4,128,4]{2,3,1,0:T(4,128)}, u32[]{:S(2)}) %copy-start.2) | copy-done | bytes 16408
  3.0 0.0 copy-start.3
  3.1 0.7 %copy-done.3 = f32[2,4,128,4]{2,3,1,0:T(4,128)S(1)} copy-done((f32[2,4,128,4]{2,3,1,0:T(4,128)S(1)}, f32[2,4,128,4]{2,3,1,0:T(4,128)}, u32[]{:S(2)}) %copy-start.3) | copy-done | bytes 16408
  3.8 25.1 %shard_map.55 = f32[5,8,8,128]{3,2,1,0:T(8,128)S(1)} custom-call(f32[5,8,8,128]{3,2,1,0:T(8,128)S(1)} %copy-done, f32[8,8,128]{2,1,0:T(8,128)S(1)} %copy-done.1, s32[4]{0:T(128)S(1)} %copy-done.4, s32[2,4,4,128]{3,2,1,0:T(4,128)S(1)} %bitcast.2, f32[2,4,4,128]{3,2,1,0:T(4,128)S(1)} %bitcast.3), custom_call_target="tpu_custom_call" | custom-call | tf_op jit(solution)/shard_map/pallas_call | solution.py:243
  28.9 0.7 %copy.7 = f32[5,8,8,128]{3,2,1,0:T(8,128)} copy(f32[5,8,8,128]{3,2,1,0:T(8,128)S(1)} %shard_map.55) | data formatting | bytes 327680
Async XLA Ops:
  0.0 0.7 %copy-start.4 = (s32[4]{0:T(128)S(1)}, s32[4]{0:T(128)}, u32[]{:S(2)}) copy-start(s32[4]{0:T(128)} %offset_ref.1) | copy-start | bytes 52
  0.7 0.9 %copy-start = (f32[5,8,8,128]{3,2,1,0:T(8,128)S(1)}, f32[5,8,8,128]{3,2,1,0:T(8,128)}, u32[]{:S(2)}) copy-start(f32[5,8,8,128]{3,2,1,0:T(8,128)} %state_ref.1) | copy-start | bytes 491524
  1.6 0.8 %copy-start.1 = (f32[8,8,128]{2,1,0:T(8,128)S(1)}, f32[8,8,128]{2,1,0:T(8,128)}, u32[]{:S(2)}) copy-start(f32[8,8,128]{2,1,0:T(8,128)} %eddy_ref.1) | copy-start | bytes 98308
  2.3 0.7 %copy-start.2 = (s32[2,4,128,4]{2,3,1,0:T(4,128)S(1)}, s32[2,4,128,4]{2,3,1,0:T(4,128)}, u32[]{:S(2)}) copy-start(s32[2,4,128,4]{2,3,1,0:T(4,128)} %param.8) | copy-start | bytes 49156
  3.0 0.7 %copy-start.3 = (f32[2,4,128,4]{2,3,1,0:T(4,128)S(1)}, f32[2,4,128,4]{2,3,1,0:T(4,128)}, u32[]{:S(2)}) copy-start(f32[2,4,128,4]{2,3,1,0:T(4,128)} %param.9) | copy-start | bytes 49156

commit v2 on v1

v2 whole, which is shorter than its diff:
```python
import functools

import jax
import jax.numpy as jnp
from jax import lax
from jax.experimental import pallas as pl
from jax.experimental.pallas import tpu as pltpu
from jax.sharding import PartitionSpec as P

AXIAL_MACH = 0.4
STEP_SIZE = 0.3
MESH = pl.DeviceIdType.MESH
STAGE = (0.5 * STEP_SIZE, 0.5 * STEP_SIZE, STEP_SIZE)
BLEND = (1.0, 2.0, 2.0, 1.0)


def build_table(index, weight):
    taps, width = index.shape
    normed = weight / jnp.sum(weight, axis=0, keepdims=True)
    source = lax.broadcasted_iota(jnp.int32, (width, width), 0)
    matrix = jnp.zeros((width, width), jnp.float32)
    for tap in range(taps):
        matrix += jnp.where(index[tap : tap + 1] == source, normed[tap : tap + 1], 0.0)
    high = matrix.astype(jnp.bfloat16)
    low = (matrix - high.astype(jnp.float32)).astype(jnp.bfloat16)
    top = jnp.concatenate([high, low], axis=1)
    bottom = jnp.concatenate([high, jnp.zeros_like(high)], axis=1)
    return jnp.concatenate([top, bottom], axis=0)


def interpolate(plane, table):
    width = plane.shape[1]
    high = plane.astype(jnp.bfloat16)
    low = (plane - high.astype(jnp.float32)).astype(jnp.bfloat16)
    both = jnp.dot(
        jnp.concatenate([high, low], axis=1), table, preferred_element_type=jnp.float32
    )
    return both[:, :width] + both[:, width:]


def kernel(
    n_circ, n_rad,
    state_hbm, eddy_hbm, offset_hbm, index_hbm, weight_hbm, out_ref,
    state_ref, eddy_ref, offset_ref, index_ref, weight_ref,
    field, total, table, plane_out, rad_bulk_out, rad_bulk_in, rad_front_out, rad_front_in,
    circ_out, circ_in,
    load_sem, plane_send, plane_recv, rad_send, rad_recv, circ_send, circ_recv, *plane_in,
):
    nvar, naxial, nradial, width = state_ref.shape
    sections = offset_ref.shape[0]
    rows = nvar * nradial
    inner = naxial - 1
    circ, rad, ax = lax.axis_index("circ"), lax.axis_index("rad"), lax.axis_index("ax")
    far = 1 - ax
    circ_up, circ_down = lax.rem(circ + 1, n_circ), lax.rem(circ + n_circ - 1, n_circ)
    has_low, has_high = rad > 0, rad < n_rad - 1

    loads = [
        pltpu.make_async_copy(source, target, load_sem.at[i])
        for i, (source, target) in enumerate(
            (
                (state_hbm, state_ref),
                (eddy_hbm, eddy_ref),
                (offset_hbm, offset_ref),
                (index_hbm.at[ax], index_ref),
                (weight_hbm.at[ax], weight_ref),
            )
        )
    ]
    for load in loads:
        load.start()

    barrier = pltpu.get_barrier_semaphore()

    def greet(device):
        pl.semaphore_signal(barrier, inc=1, device_id=device, device_id_type=MESH)

    for apart in range(n_circ):
        greet((lax.rem(circ + apart, n_circ), rad, far))
    greet((circ_up, rad, ax))
    greet((circ_down, rad, ax))

    @pl.when(has_low)
    def _():
        greet((circ, rad - 1, ax))

    @pl.when(has_high)
    def _():
        greet((circ, rad + 1, ax))

    for side, missing in ((0, jnp.logical_not(has_low)), (1, jnp.logical_not(has_high))):

        @pl.when(missing)
        def _():
            for s in range(sections):
                rad_bulk_in[s, side] = jnp.zeros((inner * nvar, width), jnp.float32)
                rad_front_in[s, side] = jnp.zeros((nvar, width), jnp.float32)

    def axial(j):
        return jnp.where(ax == 0, j, naxial - 1 - j)

    def place(j):
        return pl.ds(j * rows, rows)

    def plane_at(s, j):
        return field[s, place(j), :].reshape(nvar, nradial, width)

    for load in loads:
        load.wait()
    for j in range(naxial):
        field[0, place(j), :] = state_ref[:, axial(j)].reshape(rows, width)
    plane_out[0] = field[0, place(inner), :]

    def plane_copy(s, apart):
        return pltpu.make_async_remote_copy(
            src_ref=plane_out.at[s], dst_ref=plane_in[s].at[circ],
            send_sem=plane_send.at[s, apart], recv_sem=plane_recv.at[s, circ],
            device_id=(lax.rem(circ + apart, n_circ), rad, far), device_id_type=MESH,
        )

    def plane_arrival(s, source):
        return pltpu.make_async_remote_copy(
            src_ref=plane_out.at[s], dst_ref=plane_in[s].at[source],
            send_sem=plane_send.at[s, 0], recv_sem=plane_recv.at[s, source],
            device_id=(source, rad, far), device_id_type=MESH,
        )

    def circ_copy(s, part, side):
        return pltpu.make_async_remote_copy(
            src_ref=circ_out.at[s, part, side], dst_ref=circ_in.at[s, part, side],
            send_sem=circ_send.at[s, part, side], recv_sem=circ_recv.at[s, part, side],
            device_id=(circ_up if side == 0 else circ_down, rad, ax), device_id_type=MESH,
        )

    rad_outs, rad_ins = (rad_bulk_out, rad_front_out), (rad_bulk_in, rad_front_in)

    def rad_copy(s, part, side):
        return pltpu.make_async_remote_copy(
            src_ref=rad_outs[part].at[s, side], dst_ref=rad_ins[part].at[s, side],
            send_sem=rad_send.at[s, part, side], recv_sem=rad_recv.at[s, part, side],
            device_id=(circ, rad + 1 if side == 0 else rad - 1, ax), device_id_type=MESH,
        )

    sends_rad = (has_high, has_low)
    gets_rad = (has_low, has_high)
    spans = ((0, inner), (inner, naxial))

    def send_halos(s, part):
        first, stop = spans[part]
        tiles = (stop - first) * nvar
        cells = field[s, first * rows : stop * rows, :].reshape(tiles, nradial, width)
        lane_of = lax.broadcasted_iota(jnp.int32, cells.shape, 2)
        tile_of = lax.broadcasted_iota(jnp.int32, cells.shape, 0)
        for side, edge in ((0, width - 1), (1, 0)):
            column = jnp.broadcast_to(cells[:, :, edge : edge + 1], cells.shape)
            circ_out[s, part, side] = jnp.sum(jnp.where(lane_of == tile_of, column, 0.0), axis=0)
            circ_copy(s, part, side).start()
        for side, edge in ((0, nradial - 1), (1, 0)):
            start = first * rows + edge
            rad_outs[part][s, side] = field[s, pl.ds(start, tiles, stride=nradial), :]

            @pl.when(sends_rad[side])
            def _():
                rad_copy(s, part, side).start()

    def await_halos(s, part):
        for side in range(2):
            circ_copy(s, part, side).wait_recv()

            @pl.when(gets_rad[side])
            def _():
                rad_copy(s, part, side).wait_recv()

    lane = lax.broadcasted_iota(jnp.int32, (nvar, nradial, width), 2)
    sub = lax.broadcasted_iota(jnp.int32, (nvar, nradial, width), 1)
    zero = jnp.zeros((nvar, nradial, width), jnp.float32)
    swirl = jnp.where(ax == 1, -0.3, 0.2).astype(jnp.float32)
    toward = jnp.where(ax == 1, -0.5, 0.5).astype(jnp.float32)

    def slope_at(s, j, part, edges):
        first = (j - spans[part][0]) * nvar

        def spread(side):
            return jnp.stack(
                [
                    jnp.broadcast_to(edges[side][:, t : t + 1], (nradial, width))
                    for t in range(first, first + nvar)
                ]
            )

        def spread_rows(side):
            picked = rad_ins[part][s, side, first : first + nvar, :]
            return jnp.broadcast_to(picked[:, None, :], (nvar, nradial, width))

        q = plane_at(s, j)
        before = plane_at(s, j - 1) if j > 0 else zero
        after = plane_at(s, j + 1) if j < inner else zero
        circ_low = jnp.where(lane == 0, spread(0), pltpu.roll(q, 1, 2))
        circ_high = jnp.where(lane == width - 1, spread(1), pltpu.roll(q, width - 1, 2))
        rad_low = jnp.where(sub == 0, spread_rows(0), pltpu.roll(q, 1, 1))
        rad_high = jnp.where(sub == nradial - 1, spread_rows(1), pltpu.roll(q, nradial - 1, 1))
        diff_circ = 0.5 * (circ_high - circ_low)
        diff_axial = toward * (after - before)
        laplace = (circ_high + circ_low) + (rad_high + rad_low) + (after + before) - 6.0 * q
        slope = eddy_ref[axial(j)][None] * laplace - (swirl * diff_circ + AXIAL_MACH * diff_axial)
        diverge = diff_circ[1] + 0.5 * (rad_high[2] - rad_low[2]) + diff_axial[3]
        push = 0.5 * (rad_high[4] - rad_low[4])
        return slope - jnp.stack([diverge, diff_circ[4], push, diff_axial[4], diverge])

    def advance(s, j, slope):
        base = plane_at(0, j)
        if s == 0:
            total[j] = slope
        elif s < sections - 1:
            total[j] += BLEND[s] * slope
        else:
            out_ref[:, axial(j)] = base + (STEP_SIZE / 6.0) * (total[j] + BLEND[s] * slope)
        if s < sections - 1:
            ahead = (base + STAGE[s] * slope).reshape(rows, width)
            field[s + 1, place(j), :] = ahead
            if j == inner:
                plane_out[s + 1] = ahead

    def send_planes(s):
        for apart in reversed(range(n_circ)):
            plane_copy(s, apart).start()

    arrivals = n_circ + 2 + jnp.where(has_low, 1, 0) + jnp.where(has_high, 1, 0)
    pl.semaphore_wait(barrier, arrivals)
    send_planes(0)
    send_halos(0, 1)
    send_halos(0, 0)

    for s in range(sections):
        table[s] = build_table(index_ref[s], weight_ref[s])
        await_halos(s, 0)
        edges = [circ_in[s, 0, side] for side in range(2)]
        for j in range(inner):
            advance(s, j, slope_at(s, j, 0, edges))
        if s < sections - 1:
            send_halos(s + 1, 0)

        await_halos(s, 1)
        edges = [circ_in[s, 1, side] for side in range(2)]
        slope = slope_at(s, inner, 1, edges)
        for source in range(n_circ):
            plane_arrival(s, source).wait_recv()
        shift = jnp.where(ax == 1, offset_ref[s], n_circ - offset_ref[s])
        faced = plane_in[s][lax.rem(circ + shift, n_circ)]
        ghost = interpolate(faced, table[s]).reshape(nvar, nradial, width)
        slant = toward * ghost
        none = jnp.zeros_like(slant[0])
        slope = slope + eddy_ref[axial(inner)][None] * ghost - AXIAL_MACH * slant
        slope = slope - jnp.stack([slant[3], none, none, slant[4], slant[3]])
        advance(s, inner, slope)
        if s < sections - 1:
            send_planes(s + 1)
            send_halos(s + 1, 1)

    for s in range(sections):
        for apart in range(n_circ):
            plane_copy(s, apart).wait_send()
        for part in range(2):
            for side in range(2):
                circ_copy(s, part, side).wait_send()

                @pl.when(sends_rad[side])
                def _():
                    rad_copy(s, part, side).wait_send()


def solution(mesh):
    n_circ, n_rad = mesh.shape["circ"], mesh.shape["rad"]

    def local(state, eddy, offsets, stencil_index, stencil_weight):
        nvar, naxial, nradial, width = state.shape
        sections = offsets.shape[0]
        taps = stencil_index.shape[3]
        rows, inner = nvar * nradial, naxial - 1
        whole = pl.BlockSpec(memory_space=pltpu.HBM)
        buffer = lambda *shape: pltpu.VMEM(shape, jnp.float32)
        copies = lambda *shape: pltpu.SemaphoreType.DMA(shape)
        return pl.pallas_call(
            functools.partial(kernel, n_circ, n_rad),
            out_shape=jax.ShapeDtypeStruct(state.shape, jnp.float32),
            in_specs=[whole] * 5,
            out_specs=pl.BlockSpec(memory_space=pltpu.VMEM),
            scratch_shapes=[
                buffer(*state.shape),
                buffer(*eddy.shape),
                pltpu.SMEM((sections,), jnp.int32),
                pltpu.VMEM((sections, taps, width), jnp.int32),
                buffer(sections, taps, width),
                buffer(sections, rows * naxial, width),
                buffer(naxial, nvar, nradial, width),
                pltpu.VMEM((sections, 2 * width, 2 * width), jnp.bfloat16),
                buffer(sections, rows, width),
                buffer(sections, 2, inner * nvar, width),
                buffer(sections, 2, inner * nvar, width),
                buffer(sections, 2, nvar, width),
                buffer(sections, 2, nvar, width),
                buffer(sections, 2, 2, nradial, width),
                buffer(sections, 2, 2, nradial, width),
                copies(5),
                copies(sections, n_circ),
                copies(sections, n_circ),
                copies(sections, 2, 2),
                copies(sections, 2, 2),
                copies(sections, 2, 2),
                copies(sections, 2, 2),
                *[buffer(n_circ, rows, width) for _ in range(sections)],
            ],
            compiler_params=pltpu.CompilerParams(
                collective_id=0, has_side_effects=True, vmem_limit_bytes=60 * 1024 * 1024
            ),
        )(state, eddy, offsets, jnp.swapaxes(stencil_index, 2, 3), jnp.swapaxes(stencil_weight, 2, 3))

    return jax.shard_map(
        local,
        mesh=mesh,
        in_specs=(P(None, "ax", "rad", "circ"), P("ax", "rad", "circ"), P(), P(), P()),
        out_specs=P(None, "ax", "rad", "circ"),
        check_vma=False,
    )
```

time: 29.9 us -> 27.1 us (0.906)
  local copies, waits for them, and re-layouts: 4.43 us -> 1.59 us
    unnamed x11 -> x1, local copies, waits for them, and re-layouts: 4.43 us -> 1.59 us
where the time goes in v2:
time: 27.1 us; the launch traced here: 26.9 us
  Pallas kernels  25.3 us (93%)
  local copies, waits for them, and re-layouts  1.59 us (6%)
    pallas_call x1, Pallas kernels, local(): pl.pallas_call(functools.partial(kernel, n_circ, n_rad), out_shape=jax.Sh...  25.3 us
    unnamed x1, local copies, waits for them, and re-layouts  1.59 us

profile of v2, /device:TPU:0, one launch (start us, length us, event | category | flops | bytes accessed | tf_op | source)
XLA Modules:
  0.0 26.9 jit_solution(15258837898313229252)
XLA Ops:
  0.0 25.3 %shard_map.55 = f32[5,8,8,128]{3,2,1,0:T(8,128)} custom-call(f32[5,8,8,128]{3,2,1,0:T(8,128)} %state_hbm.1, f32[8,8,128]{2,1,0:T(8,128)} %eddy_hbm.1, s32[4]{0:T(128)} %offset_hbm.1, s32[2,4,4,128]{3,2,1,0:T(4,128)} %bitcast.2, f32[2,4,4,128]{3,2,1,0:T(4,128)} %bitcast.3), custom_call_target="tpu_custom_call" | custom-call | tf_op jit(solution)/shard_map/pallas_call | solution.py:283
  25.4 1.6 %copy.7 = f32[5,8,8,128]{3,2,1,0:T(8,128)} copy(f32[5,8,8,128]{3,2,1,0:T(8,128)} %shard_map.55) | data formatting | bytes 327680

commit v3 on v2

--- a/solution.py
+++ b/solution.py
@@ -111,11 +111,12 @@
         field[0, place(j), :] = state_ref[:, axial(j)].reshape(rows, width)
     plane_out[0] = field[0, place(inner), :]
 
-    def plane_copy(s, apart):
+    def plane_copy(s, turn):
+        target = jnp.where(circ < n_circ // 2, n_circ - 1 - turn, turn)
         return pltpu.make_async_remote_copy(
             src_ref=plane_out.at[s], dst_ref=plane_in[s].at[circ],
-            send_sem=plane_send.at[s, apart], recv_sem=plane_recv.at[s, circ],
-            device_id=(lax.rem(circ + apart, n_circ), rad, far), device_id_type=MESH,
+            send_sem=plane_send.at[s, turn], recv_sem=plane_recv.at[s, circ],
+            device_id=(target, rad, far), device_id_type=MESH,
         )
 
     def plane_arrival(s, source):
@@ -214,7 +215,7 @@
         elif s < sections - 1:
             total[j] += BLEND[s] * slope
         else:
-            out_ref[:, axial(j)] = base + (STEP_SIZE / 6.0) * (total[j] + BLEND[s] * slope)
+            out_ref[:, axial(j)] = (STEP_SIZE / 6.0) * (total[j] + BLEND[s] * slope)
         if s < sections - 1:
             ahead = (base + STAGE[s] * slope).reshape(rows, width)
             field[s + 1, place(j), :] = ahead
@@ -222,8 +223,8 @@
                 plane_out[s + 1] = ahead
 
     def send_planes(s):
-        for apart in reversed(range(n_circ)):
-            plane_copy(s, apart).start()
+        for turn in range(n_circ):
+            plane_copy(s, turn).start()
 
     arrivals = n_circ + 2 + jnp.where(has_low, 1, 0) + jnp.where(has_high, 1, 0)
     pl.semaphore_wait(barrier, arrivals)
@@ -258,8 +259,8 @@
             send_halos(s + 1, 1)
 
     for s in range(sections):
-        for apart in range(n_circ):
-            plane_copy(s, apart).wait_send()
+        for turn in range(n_circ):
+            plane_copy(s, turn).wait_send()
         for part in range(2):
             for side in range(2):
                 circ_copy(s, part, side).wait_send()
@@ -280,7 +281,7 @@
         whole = pl.BlockSpec(memory_space=pltpu.HBM)
         buffer = lambda *shape: pltpu.VMEM(shape, jnp.float32)
         copies = lambda *shape: pltpu.SemaphoreType.DMA(shape)
-        return pl.pallas_call(
+        step = pl.pallas_call(
             functools.partial(kernel, n_circ, n_rad),
             out_shape=jax.ShapeDtypeStruct(state.shape, jnp.float32),
             in_specs=[whole] * 5,
@@ -314,6 +315,7 @@
                 collective_id=0, has_side_effects=True, vmem_limit_bytes=60 * 1024 * 1024
             ),
         )(state, eddy, offsets, jnp.swapaxes(stencil_index, 2, 3), jnp.swapaxes(stencil_weight, 2, 3))
+        return state + step
 
     return jax.shard_map(
         local,

time: 27.1 us -> 27.1 us (level)
  other arithmetic: 0 us -> 1.6 us
  local copies, waits for them, and re-layouts: 1.59 us -> 0.01 us
    add x0 -> x1, other arithmetic: none -> 1.6 us  [local(): return state + step]
    unnamed x1 -> x2, local copies, waits for them, and re-layouts: 1.59 us -> 0.01 us
where the time goes in v3:
time: 27.1 us; the launch traced here: 27 us
  Pallas kernels  25.3 us (93%)
  other arithmetic  1.6 us (6%)
    pallas_call x1, Pallas kernels, local(): pl.pallas_call(functools.partial(kernel, n_circ, n_rad), out_shape=jax.Sh...  25.3 us
    add x1, other arithmetic, local(): return state + step  1.6 us

profile of v3, /device:TPU:0, one launch (start us, length us, event | category | flops | bytes accessed | tf_op | source)
XLA Modules:
  0.0 27.0 jit_solution(9276193118421838916)
XLA Ops:
  0.0 0.0 copy-start
  0.0 25.3 %shard_map.55 = f32[5,8,8,128]{3,2,1,0:T(8,128)} custom-call(f32[5,8,8,128]{3,2,1,0:T(8,128)} %state_hbm.1, f32[8,8,128]{2,1,0:T(8,128)} %eddy_hbm.1, s32[4]{0:T(128)} %offset_hbm.1, s32[2,4,4,128]{3,2,1,0:T(4,128)} %bitcast.2, f32[2,4,4,128]{3,2,1,0:T(4,128)} %bitcast.3), custom_call_target="tpu_custom_call" | custom-call | tf_op jit(solution)/shard_map/pallas_call | solution.py:284
  25.3 0.0 copy-done
  25.4 1.6 %add.3 = f32[5,8,8,128]{3,2,1,0:T(8,128)} add(f32[5,8,8,128]{3,2,1,0:T(8,128)S(1)} %copy-done, f32[5,8,8,128]{3,2,1,0:T(8,128)} %shard_map.55) | non-fusion elementwise | flops 40960 | bytes 491520 | tf_op jit(solution)/shard_map/add | solution.py:318
Async XLA Ops:
  0.0 25.3 %copy-start = (f32[5,8,8,128]{3,2,1,0:T(8,128)S(1)}, f32[5,8,8,128]{3,2,1,0:T(8,128)}, u32[]{:S(2)}) copy-start(f32[5,8,8,128]{3,2,1,0:T(8,128)} %state_hbm.1) | copy-start | bytes 491524

commit v4 on v3

--- a/solution.py
+++ b/solution.py
@@ -215,7 +215,7 @@
         elif s < sections - 1:
             total[j] += BLEND[s] * slope
         else:
-            out_ref[:, axial(j)] = (STEP_SIZE / 6.0) * (total[j] + BLEND[s] * slope)
+            out_ref[:, axial(j)] = base + (STEP_SIZE / 6.0) * (total[j] + BLEND[s] * slope)
         if s < sections - 1:
             ahead = (base + STAGE[s] * slope).reshape(rows, width)
             field[s + 1, place(j), :] = ahead
@@ -283,7 +283,7 @@
         copies = lambda *shape: pltpu.SemaphoreType.DMA(shape)
         step = pl.pallas_call(
             functools.partial(kernel, n_circ, n_rad),
-            out_shape=jax.ShapeDtypeStruct(state.shape, jnp.float32),
+            out_shape=pltpu.VMEM(state.shape, jnp.float32),
             in_specs=[whole] * 5,
             out_specs=pl.BlockSpec(memory_space=pltpu.VMEM),
             scratch_shapes=[
@@ -315,7 +315,7 @@
                 collective_id=0, has_side_effects=True, vmem_limit_bytes=60 * 1024 * 1024
             ),
         )(state, eddy, offsets, jnp.swapaxes(stencil_index, 2, 3), jnp.swapaxes(stencil_weight, 2, 3))
-        return state + step
+        return step
 
     return jax.shard_map(
         local,

time: 27.1 us -> 25.5 us (0.941)
  other arithmetic: 1.6 us -> 0 us
  local copies, waits for them, and re-layouts: 0.01 us -> 0.67 us
  Pallas kernels: 25.3 us -> 24.7 us
    add x1 -> x0, other arithmetic: 1.6 us -> none  [local(): return state + step]
    unnamed x2 -> x1, local copies, waits for them, and re-layouts: 0.01 us -> 0.67 us
    pallas_call x1, Pallas kernels: 25.3 us -> 24.7 us  [local(): pl.pallas_call(functools.partial(kernel, n_circ, n_rad), out_shape=pltpu....]
where the time goes in v4:
time: 25.5 us; the launch traced here: 25.3 us
  Pallas kernels  24.7 us (97%)
  local copies, waits for them, and re-layouts  0.67 us (3%)
    pallas_call x1, Pallas kernels, local(): pl.pallas_call(functools.partial(kernel, n_circ, n_rad), out_shape=pltpu....  24.7 us
    unnamed x1, local copies, waits for them, and re-layouts  0.67 us

profile of v4, /device:TPU:0, one launch (start us, length us, event | category | flops | bytes accessed | tf_op | source)
XLA Modules:
  0.0 25.3 jit_solution(11539700121868298217)
XLA Ops:
  0.0 24.7 %shard_map.55 = f32[5,8,8,128]{3,2,1,0:T(8,128)S(1)} custom-call(f32[5,8,8,128]{3,2,1,0:T(8,128)} %state_hbm.1, f32[8,8,128]{2,1,0:T(8,128)} %eddy_hbm.1, s32[4]{0:T(128)} %offset_hbm.1, s32[2,4,4,128]{3,2,1,0:T(4,128)} %bitcast.2, f32[2,4,4,128]{3,2,1,0:T(4,128)} %bitcast.3), custom_call_target="tpu_custom_call" | custom-call | tf_op jit(solution)/shard_map/pallas_call | solution.py:284
  24.7 0.7 %copy.7 = f32[5,8,8,128]{3,2,1,0:T(8,128)} copy(f32[5,8,8,128]{3,2,1,0:T(8,128)S(1)} %shard_map.55) | data formatting | bytes 327680

commit v5 on v4

--- a/solution.py
+++ b/solution.py
@@ -42,7 +42,7 @@
     n_circ, n_rad,
     state_hbm, eddy_hbm, offset_hbm, index_hbm, weight_hbm, out_ref,
     state_ref, eddy_ref, offset_ref, index_ref, weight_ref,
-    field, total, table, plane_out, rad_bulk_out, rad_bulk_in, rad_front_out, rad_front_in,
+    field, slopes, total, table, plane_out, rad_bulk_out, rad_bulk_in, rad_front_out, rad_front_in,
     circ_out, circ_in,
     load_sem, plane_send, plane_recv, rad_send, rad_recv, circ_send, circ_recv, *plane_in,
 ):
@@ -55,6 +55,24 @@
     circ_up, circ_down = lax.rem(circ + 1, n_circ), lax.rem(circ + n_circ - 1, n_circ)
     has_low, has_high = rad > 0, rad < n_rad - 1
 
+    barrier = pltpu.get_barrier_semaphore()
+
+    def greet(device):
+        pl.semaphore_signal(barrier, inc=1, device_id=device, device_id_type=MESH)
+
+    for apart in range(n_circ):
+        greet((lax.rem(circ + apart, n_circ), rad, far))
+    greet((circ_up, rad, ax))
+    greet((circ_down, rad, ax))
+
+    @pl.when(has_low)
+    def _():
+        greet((circ, rad - 1, ax))
+
+    @pl.when(has_high)
+    def _():
+        greet((circ, rad + 1, ax))
+
     loads = [
         pltpu.make_async_copy(source, target, load_sem.at[i])
         for i, (source, target) in enumerate(
@@ -69,24 +87,6 @@
     ]
     for load in loads:
         load.start()
-
-    barrier = pltpu.get_barrier_semaphore()
-
-    def greet(device):
-        pl.semaphore_signal(barrier, inc=1, device_id=device, device_id_type=MESH)
-
-    for apart in range(n_circ):
-        greet((lax.rem(circ + apart, n_circ), rad, far))
-    greet((circ_up, rad, ax))
-    greet((circ_down, rad, ax))
-
-    @pl.when(has_low)
-    def _():
-        greet((circ, rad - 1, ax))
-
-    @pl.when(has_high)
-    def _():
-        greet((circ, rad + 1, ax))
 
     for side, missing in ((0, jnp.logical_not(has_low)), (1, jnp.logical_not(has_high))):
 
@@ -178,28 +178,19 @@
     swirl = jnp.where(ax == 1, -0.3, 0.2).astype(jnp.float32)
     toward = jnp.where(ax == 1, -0.5, 0.5).astype(jnp.float32)
 
-    def slope_at(s, j, part, edges):
-        first = (j - spans[part][0]) * nvar
-
-        def spread(side):
-            return jnp.stack(
-                [
-                    jnp.broadcast_to(edges[side][:, t : t + 1], (nradial, width))
-                    for t in range(first, first + nvar)
-                ]
-            )
-
-        def spread_rows(side):
-            picked = rad_ins[part][s, side, first : first + nvar, :]
-            return jnp.broadcast_to(picked[:, None, :], (nvar, nradial, width))
-
+    at_low, at_high = lane[0] == 0, lane[0] == width - 1
+    at_under, at_over = sub[0] == 0, sub[0] == nradial - 1
+    half = lambda where: jnp.where(where, 0.5, 0.0).astype(jnp.float32)
+    half_low, half_high, half_under, half_over = map(half, (at_low, at_high, at_under, at_over))
+
+    def inside(s, j):
         q = plane_at(s, j)
         before = plane_at(s, j - 1) if j > 0 else zero
         after = plane_at(s, j + 1) if j < inner else zero
-        circ_low = jnp.where(lane == 0, spread(0), pltpu.roll(q, 1, 2))
-        circ_high = jnp.where(lane == width - 1, spread(1), pltpu.roll(q, width - 1, 2))
-        rad_low = jnp.where(sub == 0, spread_rows(0), pltpu.roll(q, 1, 1))
-        rad_high = jnp.where(sub == nradial - 1, spread_rows(1), pltpu.roll(q, nradial - 1, 1))
+        circ_low = jnp.where(lane == 0, 0.0, pltpu.roll(q, 1, 2))
+        circ_high = jnp.where(lane == width - 1, 0.0, pltpu.roll(q, width - 1, 2))
+        rad_low = jnp.where(sub == 0, 0.0, pltpu.roll(q, 1, 1))
+        rad_high = jnp.where(sub == nradial - 1, 0.0, pltpu.roll(q, nradial - 1, 1))
         diff_circ = 0.5 * (circ_high - circ_low)
         diff_axial = toward * (after - before)
         laplace = (circ_high + circ_low) + (rad_high + rad_low) + (after + before) - 6.0 * q
@@ -207,6 +198,37 @@
         diverge = diff_circ[1] + 0.5 * (rad_high[2] - rad_low[2]) + diff_axial[3]
         push = 0.5 * (rad_high[4] - rad_low[4])
         return slope - jnp.stack([diverge, diff_circ[4], push, diff_axial[4], diverge])
+
+    def from_halos(s, j, part, edges):
+        first = (j - spans[part][0]) * nvar
+        eddy = eddy_ref[axial(j)]
+        by_low = jnp.where(at_low, eddy + 0.5 * swirl, 0.0)
+        by_high = jnp.where(at_high, eddy - 0.5 * swirl, 0.0)
+        by_under = jnp.where(at_under, eddy, 0.0)
+        by_over = jnp.where(at_over, eddy, 0.0)
+
+        def column(side, v):
+            t = first + v
+            return jnp.broadcast_to(edges[side][:, t : t + 1], (nradial, width))
+
+        def row(side, v):
+            picked = rad_ins[part][s, side, first + v : first + v + 1, :]
+            return jnp.broadcast_to(picked, (nradial, width))
+
+        low, high = ([column(side, v) for v in range(nvar)] for side in range(2))
+        under, over = ([row(side, v) for v in range(nvar)] for side in range(2))
+        added = [
+            (by_low * low[v] + by_high * high[v]) + (by_under * under[v] + by_over * over[v])
+            for v in range(nvar)
+        ]
+        spread = (half_low * low[1] - half_high * high[1]) + (
+            half_under * under[2] - half_over * over[2]
+        )
+        added[0] += spread
+        added[1] += half_low * low[4] - half_high * high[4]
+        added[2] += half_under * under[4] - half_over * over[4]
+        added[4] += spread
+        return jnp.stack(added)
 
     def advance(s, j, slope):
         base = plane_at(0, j)
@@ -234,16 +256,18 @@
 
     for s in range(sections):
         table[s] = build_table(index_ref[s], weight_ref[s])
+        for j in range(naxial):
+            slopes[j] = inside(s, j)
         await_halos(s, 0)
         edges = [circ_in[s, 0, side] for side in range(2)]
         for j in range(inner):
-            advance(s, j, slope_at(s, j, 0, edges))
+            advance(s, j, slopes[j] + from_halos(s, j, 0, edges))
         if s < sections - 1:
             send_halos(s + 1, 0)
 
         await_halos(s, 1)
         edges = [circ_in[s, 1, side] for side in range(2)]
-        slope = slope_at(s, inner, 1, edges)
+        slope = slopes[inner] + from_halos(s, inner, 1, edges)
         for source in range(n_circ):
             plane_arrival(s, source).wait_recv()
         shift = jnp.where(ax == 1, offset_ref[s], n_circ - offset_ref[s])
@@ -293,6 +317,7 @@
                 pltpu.VMEM((sections, taps, width), jnp.int32),
                 buffer(sections, taps, width),
                 buffer(sections, rows * naxial, width),
+                buffer(naxial, nvar, nradial, width),
                 buffer(naxial, nvar, nradial, width),
                 pltpu.VMEM((sections, 2 * width, 2 * width), jnp.bfloat16),
                 buffer(sections, rows, width),

time: 25.5 us -> 25.3 us (level)
  no operation moved by 1% of the time
where the time goes in v5:
time: 25.3 us; the launch traced here: 25.1 us
  Pallas kernels  24.5 us (97%)
  local copies, waits for them, and re-layouts  0.67 us (3%)
    pallas_call x1, Pallas kernels, local(): pl.pallas_call(functools.partial(kernel, n_circ, n_rad), out_shape=pltpu....  24.5 us
    unnamed x1, local copies, waits for them, and re-layouts  0.67 us

profile of v5, /device:TPU:0, one launch (start us, length us, event | category | flops | bytes accessed | tf_op | source)
XLA Modules:
  0.0 25.1 jit_solution(18099731400360165035)
XLA Ops:
  0.0 24.5 %shard_map.55 = f32[5,8,8,128]{3,2,1,0:T(8,128)S(1)} custom-call(f32[5,8,8,128]{3,2,1,0:T(8,128)} %state_hbm.1, f32[8,8,128]{2,1,0:T(8,128)} %eddy_hbm.1, s32[4]{0:T(128)} %offset_hbm.1, s32[2,4,4,128]{3,2,1,0:T(4,128)} %bitcast.2, f32[2,4,4,128]{3,2,1,0:T(4,128)} %bitcast.3), custom_call_target="tpu_custom_call" | custom-call | tf_op jit(solution)/shard_map/pallas_call | solution.py:308
  24.5 0.7 %copy.7 = f32[5,8,8,128]{3,2,1,0:T(8,128)} copy(f32[5,8,8,128]{3,2,1,0:T(8,128)S(1)} %shard_map.55) | data formatting | bytes 327680

commit v6 on v5

--- a/solution.py
+++ b/solution.py
@@ -10,8 +10,6 @@
 AXIAL_MACH = 0.4
 STEP_SIZE = 0.3
 MESH = pl.DeviceIdType.MESH
-STAGE = (0.5 * STEP_SIZE, 0.5 * STEP_SIZE, STEP_SIZE)
-BLEND = (1.0, 2.0, 2.0, 1.0)
 
 
 def build_table(index, weight):
@@ -44,7 +42,7 @@
     state_ref, eddy_ref, offset_ref, index_ref, weight_ref,
     field, slopes, total, table, plane_out, rad_bulk_out, rad_bulk_in, rad_front_out, rad_front_in,
     circ_out, circ_in,
-    load_sem, plane_send, plane_recv, rad_send, rad_recv, circ_send, circ_recv, *plane_in,
+    load_sem, plane_send, plane_recv, rad_send, rad_recv, circ_send, circ_recv, plane_in,
 ):
     nvar, naxial, nradial, width = state_ref.shape
     sections = offset_ref.shape[0]
@@ -114,14 +112,14 @@
     def plane_copy(s, turn):
         target = jnp.where(circ < n_circ // 2, n_circ - 1 - turn, turn)
         return pltpu.make_async_remote_copy(
-            src_ref=plane_out.at[s], dst_ref=plane_in[s].at[circ],
+            src_ref=plane_out.at[s], dst_ref=plane_in.at[s, circ],
             send_sem=plane_send.at[s, turn], recv_sem=plane_recv.at[s, circ],
             device_id=(target, rad, far), device_id_type=MESH,
         )
 
     def plane_arrival(s, source):
         return pltpu.make_async_remote_copy(
-            src_ref=plane_out.at[s], dst_ref=plane_in[s].at[source],
+            src_ref=plane_out.at[s], dst_ref=plane_in.at[s, source],
             send_sem=plane_send.at[s, 0], recv_sem=plane_recv.at[s, source],
             device_id=(source, rad, far), device_id_type=MESH,
         )
@@ -231,18 +229,13 @@
         return jnp.stack(added)
 
     def advance(s, j, slope):
-        base = plane_at(0, j)
-        if s == 0:
-            total[j] = slope
-        elif s < sections - 1:
-            total[j] += BLEND[s] * slope
-        else:
-            out_ref[:, axial(j)] = base + (STEP_SIZE / 6.0) * (total[j] + BLEND[s] * slope)
-        if s < sections - 1:
-            ahead = (base + STAGE[s] * slope).reshape(rows, width)
-            field[s + 1, place(j), :] = ahead
-            if j == inner:
-                plane_out[s + 1] = ahead
+        blend = jnp.where((s == 0) | (s == sections - 1), 1.0, 2.0).astype(jnp.float32)
+        reach = jnp.where(s < sections - 2, 0.5 * STEP_SIZE, STEP_SIZE).astype(jnp.float32)
+        total[j] += blend * slope
+        ahead = (plane_at(0, j) + reach * slope).reshape(rows, width)
+        field[s + 1, place(j), :] = ahead
+        if j == inner:
+            plane_out[s + 1] = ahead
 
     def send_planes(s):
         for turn in range(n_circ):
@@ -254,7 +247,7 @@
     send_halos(0, 1)
     send_halos(0, 0)
 
-    for s in range(sections):
+    def section(s, carry):
         table[s] = build_table(index_ref[s], weight_ref[s])
         for j in range(naxial):
             slopes[j] = inside(s, j)
@@ -262,7 +255,9 @@
         edges = [circ_in[s, 0, side] for side in range(2)]
         for j in range(inner):
             advance(s, j, slopes[j] + from_halos(s, j, 0, edges))
-        if s < sections - 1:
+
+        @pl.when(s < sections - 1)
+        def _():
             send_halos(s + 1, 0)
 
         await_halos(s, 1)
@@ -271,18 +266,31 @@
         for source in range(n_circ):
             plane_arrival(s, source).wait_recv()
         shift = jnp.where(ax == 1, offset_ref[s], n_circ - offset_ref[s])
-        faced = plane_in[s][lax.rem(circ + shift, n_circ)]
+        facing = lax.rem(circ + shift, n_circ)
+        faced = plane_in[s, 0]
+        for source in range(1, n_circ):
+            faced = jnp.where(facing == source, plane_in[s, source], faced)
         ghost = interpolate(faced, table[s]).reshape(nvar, nradial, width)
         slant = toward * ghost
         none = jnp.zeros_like(slant[0])
         slope = slope + eddy_ref[axial(inner)][None] * ghost - AXIAL_MACH * slant
         slope = slope - jnp.stack([slant[3], none, none, slant[4], slant[3]])
         advance(s, inner, slope)
-        if s < sections - 1:
+
+        @pl.when(s < sections - 1)
+        def _():
             send_planes(s + 1)
             send_halos(s + 1, 1)
 
-    for s in range(sections):
+        return carry
+
+    total[...] = jnp.zeros_like(total)
+    lax.fori_loop(0, sections, section, 0)
+
+    for j in range(naxial):
+        out_ref[:, axial(j)] = plane_at(0, j) + (STEP_SIZE / 6.0) * total[j]
+
+    def finish(s, carry):
         for turn in range(n_circ):
             plane_copy(s, turn).wait_send()
         for part in range(2):
@@ -292,6 +300,10 @@
                 @pl.when(sends_rad[side])
                 def _():
                     rad_copy(s, part, side).wait_send()
+
+        return carry
+
+    lax.fori_loop(0, sections, finish, 0)
 
 
 def solution(mesh):
@@ -316,11 +328,11 @@
                 pltpu.SMEM((sections,), jnp.int32),
                 pltpu.VMEM((sections, taps, width), jnp.int32),
                 buffer(sections, taps, width),
-                buffer(sections, rows * naxial, width),
+                buffer(sections + 1, rows * naxial, width),
                 buffer(naxial, nvar, nradial, width),
                 buffer(naxial, nvar, nradial, width),
                 pltpu.VMEM((sections, 2 * width, 2 * width), jnp.bfloat16),
-                buffer(sections, rows, width),
+                buffer(sections + 1, rows, width),
                 buffer(sections, 2, inner * nvar, width),
                 buffer(sections, 2, inner * nvar, width),
                 buffer(sections, 2, nvar, width),
@@ -334,7 +346,7 @@
                 copies(sections, 2, 2),
                 copies(sections, 2, 2),
                 copies(sections, 2, 2),
-                *[buffer(n_circ, rows, width) for _ in range(sections)],
+                buffer(sections, n_circ, rows, width),
             ],
             compiler_params=pltpu.CompilerParams(
                 collective_id=0, has_side_effects=True, vmem_limit_bytes=60 * 1024 * 1024

time: 25.3 us -> 25.4 us (level)
  no operation moved by 1% of the time
where the time goes in v6:
time: 25.4 us; the launch traced here: 25.2 us
  Pallas kernels  24.5 us (96%)
  local copies, waits for them, and re-layouts  0.67 us (3%)
    pallas_call x1, Pallas kernels, local(): pl.pallas_call(functools.partial(kernel, n_circ, n_rad), out_shape=pltpu....  24.5 us
    unnamed x1, local copies, waits for them, and re-layouts  0.67 us

profile of v6, /device:TPU:0, one launch (start us, length us, event | category | flops | bytes accessed | tf_op | source)
XLA Modules:
  0.0 25.2 jit_solution(2667060742079306282)
XLA Ops:
  0.0 24.5 %shard_map.55 = f32[5,8,8,128]{3,2,1,0:T(8,128)S(1)} custom-call(f32[5,8,8,128]{3,2,1,0:T(8,128)} %state_hbm.1, f32[8,8,128]{2,1,0:T(8,128)} %eddy_hbm.1, s32[4]{0:T(128)} %offset_hbm.1, s32[2,4,4,128]{3,2,1,0:T(4,128)} %bitcast.2, f32[2,4,4,128]{3,2,1,0:T(4,128)} %bitcast.3), custom_call_target="tpu_custom_call" | custom-call | tf_op jit(solution)/shard_map/pallas_call | solution.py:320
  24.6 0.7 %copy.7 = f32[5,8,8,128]{3,2,1,0:T(8,128)} copy(f32[5,8,8,128]{3,2,1,0:T(8,128)S(1)} %shard_map.55) | data formatting | bytes 327680

commit v7 on v6

--- a/solution.py
+++ b/solution.py
@@ -256,10 +256,6 @@
         for j in range(inner):
             advance(s, j, slopes[j] + from_halos(s, j, 0, edges))
 
-        @pl.when(s < sections - 1)
-        def _():
-            send_halos(s + 1, 0)
-
         await_halos(s, 1)
         edges = [circ_in[s, 1, side] for side in range(2)]
         slope = slopes[inner] + from_halos(s, inner, 1, edges)
@@ -281,6 +277,7 @@
         def _():
             send_planes(s + 1)
             send_halos(s + 1, 1)
+            send_halos(s + 1, 0)
 
         return carry
 

time: 25.4 us -> 26 us (1.024)
  Pallas kernels: 24.5 us -> 25.2 us
    pallas_call x1, Pallas kernels: 24.5 us -> 25.2 us  [local(): pl.pallas_call(functools.partial(kernel, n_circ, n_rad), out_shape=pltpu....]
where the time goes in v7:
time: 26 us; the launch traced here: 25.8 us
  Pallas kernels  25.2 us (97%)
  local copies, waits for them, and re-layouts  0.67 us (3%)
    pallas_call x1, Pallas kernels, local(): pl.pallas_call(functools.partial(kernel, n_circ, n_rad), out_shape=pltpu....  25.2 us
    unnamed x1, local copies, waits for them, and re-layouts  0.67 us

profile of v7, /device:TPU:0, one launch (start us, length us, event | category | flops | bytes accessed | tf_op | source)
XLA Modules:
  0.0 25.8 jit_solution(3556731820927069160)
XLA Ops:
  0.0 25.2 %shard_map.55 = f32[5,8,8,128]{3,2,1,0:T(8,128)S(1)} custom-call(f32[5,8,8,128]{3,2,1,0:T(8,128)} %state_hbm.1, f32[8,8,128]{2,1,0:T(8,128)} %eddy_hbm.1, s32[4]{0:T(128)} %offset_hbm.1, s32[2,4,4,128]{3,2,1,0:T(4,128)} %bitcast.2, f32[2,4,4,128]{3,2,1,0:T(4,128)} %bitcast.3), custom_call_target="tpu_custom_call" | custom-call | tf_op jit(solution)/shard_map/pallas_call | solution.py:317
  25.2 0.7 %copy.7 = f32[5,8,8,128]{3,2,1,0:T(8,128)} copy(f32[5,8,8,128]{3,2,1,0:T(8,128)S(1)} %shard_map.55) | data formatting | bytes 327680
